TPU v7x, 32 devices: a whole 2x2x4 slice. The times are simulated.
32 devices in a mesh: section: 2 (over core), tensor: 4 (over y, x), dp: 4 (over z).
Axes of the slice: x: 2, y: 2, z: 4, core: 2. Of those that a mesh axis runs over, the one named last changes fastest.
Arguments:
- activations: bfloat16 [2, 1, 1024, 1024], P(None, None, ('dp', 'tensor')), may hold values from -6 to 6
- lengths: int32 [2, 1, 8], replicated, may hold values from 1 to 768, as said below
- projection: bfloat16 [2, 1024, 3, 1024], P('section', None, None, 'tensor'), may hold values from -0.1875 to 0.1875
- output_weight: bfloat16 [2, 1024, 1024], P('section', 'tensor'), may hold values from -0.1875 to 0.1875
- expansion: bfloat16 [2, 1024, 2, 4096], P('section', None, None, 'tensor'), may hold values from -0.1875 to 0.1875
- reduction: bfloat16 [2, 4096, 1024], P('section', 'tensor'), may hold values from -0.09375 to 0.09375
- query_scale: float32 [2, 1024], P('section', 'tensor'), may hold values from 0.7 to 1.6
- unit_scales: float32 [2, 2, 4096], P('section', None, 'tensor'), may hold values from 0.5 to 2
- alphas: float32 [2, 2, 1024], P('section'), may hold values from 0.2 to 0.8
- cotangent: bfloat16 [2, 1, 1024, 1024], P(None, None, ('dp', 'tensor')), may hold values from -6 to 6
Outputs:
- layer_output: bfloat16 [2, 2, 1, 1024, 1024], P('section', None, None, ('dp', 'tensor'))
- input_gradient: bfloat16 [2, 2, 1, 1024, 1024], P('section', None, None, ('dp', 'tensor'))
- projection_gradient: float32 [2, 1024, 3, 1024], P('section', None, None, 'tensor')
- output_gradient: float32 [2, 1024, 1024], P('section', 'tensor')
- expansion_gradient: float32 [2, 1024, 2, 4096], P('section', None, None, 'tensor')
- reduction_gradient: float32 [2, 4096, 1024], P('section', 'tensor')
- query_scale_gradient: float32 [2, 1024], P('section', 'tensor')
- unit_scales_gradient: float32 [2, 2, 4096], P('section', None, 'tensor')
- alphas_gradient: float32 [2, 2, 1024], P('section')
Inputs may be any that keep to these rules, and one draw needn't show every extreme that they name: `lengths`: the sequences of a row lie in order from slot 0; the slots after the last one are padding.
All inputs are finite; a program needn't handle non-finite values.
Results may differ from a plain program's by a relative error of at most 0.04.
Values may be sent and summed in bfloat16 or wider, within the bound.
A program may use at most 192 MiB of HBM per device.

v0:
```python
import math

import jax
import jax.numpy as jnp
from jax import lax
from jax.sharding import PartitionSpec as P

HDIM = 64


def from_behind(value, axis, steps):
    count = lax.axis_size(axis)
    initial, last = (max(0, -steps), min(count, count - steps))
    return lax.ppermute(value, axis, [(source, source + steps) for source in range(initial, last)])


def normed(v):
    return v * lax.rsqrt(jnp.mean(v * v, axis=-1, keepdims=True) + 1e-06)


def unit_heads(v):
    return v * lax.rsqrt(jnp.sum(v * v, axis=-1, keepdims=True) + 1e-06)


def frequencies(half):
    return jnp.exp(jnp.arange(half, dtype=jnp.float32) * (-2.0 * math.log(10000.0) / (2 * half)))


def rotate(view, angle):
    half = view.shape[-1] // 2
    cosine = jnp.cos(angle)[..., None, :]
    sine = jnp.sin(angle)[..., None, :]
    front = view[..., :half]
    back = view[..., half:]
    return jnp.concatenate([front * cosine - back * sine, back * cosine + front * sine], axis=-1)


def shaped(projected, scale, angle, heads):
    inner = projected.shape[-1] // 3
    lead = projected.shape[:-1]

    def turned(piece):
        view = piece.reshape(lead + (heads, inner // heads))
        return unit_heads(rotate(view, angle)).reshape(lead + (inner,)) * scale

    return (
        turned(projected[..., :inner]),
        turned(projected[..., inner : 2 * inner]),
        projected[..., 2 * inner :],
    )


def layout(lengths_row, slots):
    ends = jnp.cumsum(lengths_row, dtype=jnp.int32)
    index = jnp.arange(slots, dtype=jnp.int32)
    after = index[:, None] >= ends[None, :]
    segment = jnp.sum(after.astype(jnp.int32), axis=1, dtype=jnp.int32)
    begin = jnp.sum(jnp.where(after, lengths_row[None, :], 0), axis=1, dtype=jnp.int32)
    inside = index < ends[-1]
    segment = jnp.where(inside, segment, lengths_row.shape[0] + index)
    position = jnp.where(inside, index - begin, 0)
    return (segment, position)


def blend(base, branch, alpha):
    return normed(base + alpha * (normed(branch) - base))


def activate(expanded, scales):
    half = expanded.shape[-1] // 2
    return expanded[..., :half] * scales[0] * jax.nn.silu(expanded[..., half:] * scales[1])


def placing(lengths_now, local):
    slots = local * lax.axis_size("dp")
    start_here = lax.axis_index("dp") * local
    segment_all, position_all = jax.vmap(lambda row: layout(row, slots))(lengths_now)
    segment_here = lax.dynamic_slice_in_dim(segment_all, start_here, local, 1)
    position_here = lax.dynamic_slice_in_dim(position_all, start_here, local, 1)
    index_here = start_here + jnp.arange(local, dtype=jnp.int32)
    every = jnp.arange(slots, dtype=jnp.int32)
    allowed = (segment_here[:, :, None] == segment_all[:, None, :]) & (
        every[None, None, :] <= index_here[None, :, None]
    )
    angle = position_here.astype(jnp.float32)[..., None] * frequencies(HDIM // 2)
    return (allowed, angle)


def scored(query, key_all, allowed, heads):
    rows, local, inner = query.shape
    depth = inner // heads
    query_heads = query.reshape(rows, local, heads, depth)
    key_heads = key_all.reshape(rows, key_all.shape[1], heads, depth)
    raw = jnp.einsum(
        "rqhe,rkhe->rhqk", query_heads, key_heads, preferred_element_type=jnp.float32
    ) * math.sqrt(depth)
    return jnp.where(allowed[:, None], raw, -1e30)


def forward(stream, lengths_now, weights):
    projection, output_weight, expansion, reduction, query_scale, unit_scales, alphas = weights
    rows, part, width = stream.shape
    inner = output_weight.shape[0]
    heads = inner // HDIM
    hidden_width = reduction.shape[0]
    gathered = lax.all_gather(stream.astype(jnp.bfloat16), "tensor", axis=1, tiled=True)
    local = gathered.shape[1]
    allowed, angle = placing(lengths_now, local)
    projected = jnp.einsum(
        "rsd,dc->rsc",
        gathered,
        projection.reshape(width, 3 * inner),
        preferred_element_type=jnp.float32,
    )
    query, key, value = shaped(projected, query_scale, angle, heads)
    query_low = query.astype(jnp.bfloat16)
    key_low = key.astype(jnp.bfloat16)
    value_low = value.astype(jnp.bfloat16)
    key_all, value_all = (
        lax.all_gather(key_low, "dp", axis=1, tiled=True),
        lax.all_gather(value_low, "dp", axis=1, tiled=True),
    )
    scores = scored(query_low, key_all, allowed, heads)
    highest = jnp.max(scores, axis=-1, keepdims=True)
    lifted = jnp.exp(scores - highest)
    total = jnp.sum(lifted, axis=-1, keepdims=True)
    log_total = highest + jnp.log(total)
    probs_low = (lifted / total).astype(jnp.bfloat16)
    value_heads = value_all.reshape(rows, value_all.shape[1], heads, HDIM)
    mixed = jnp.einsum(
        "rhqk,rkhe->rqhe", probs_low, value_heads, preferred_element_type=jnp.float32
    )
    attended = mixed.reshape(rows, local, inner).astype(jnp.bfloat16)
    partial_branch = jnp.einsum(
        "rsc,cd->rsd", attended, output_weight, preferred_element_type=jnp.float32
    )
    branch = lax.psum_scatter(partial_branch, "tensor", scatter_dimension=1, tiled=True)
    middle = blend(stream, branch, alphas[0])
    middle_all = lax.all_gather(middle.astype(jnp.bfloat16), "tensor", axis=1, tiled=True)
    expanded = jnp.einsum(
        "rsd,dc->rsc",
        middle_all,
        expansion.reshape(width, 2 * hidden_width),
        preferred_element_type=jnp.float32,
    )
    hidden = activate(expanded, unit_scales).astype(jnp.bfloat16)
    partial_feed = jnp.einsum("rsf,fd->rsd", hidden, reduction, preferred_element_type=jnp.float32)
    feed = lax.psum_scatter(partial_feed, "tensor", scatter_dimension=1, tiled=True)
    result = blend(middle, feed, alphas[1])
    kept = dict(
        stream=stream,
        gathered=gathered,
        projected=projected,
        query=query_low,
        key=key_low,
        value=value_low,
        log_total=log_total,
        attended=attended,
        branch=branch,
        middle=middle,
        middle_all=middle_all,
        expanded=expanded,
        hidden=hidden,
        feed=feed,
        lengths=lengths_now,
    )
    kept = dict(kept, key_all=key_all, value_all=value_all)
    return (result, kept)


def backward(slope, kept, weights):
    projection, output_weight, expansion, reduction, query_scale, unit_scales, alphas = weights
    rows, part, width = slope.shape
    inner = output_weight.shape[0]
    heads = inner // HDIM
    hidden_width = reduction.shape[0]
    _, pull_feed = jax.vjp(blend, kept["middle"], kept["feed"], alphas[1])
    middle_slope, feed_slope, alpha_feed = pull_feed(slope)
    feed_all = lax.all_gather(feed_slope.astype(jnp.bfloat16), "tensor", axis=1, tiled=True)
    reduction_grad = jnp.einsum(
        "rsf,rsd->fd", kept["hidden"], feed_all, preferred_element_type=jnp.float32
    )
    hidden_slope = jnp.einsum(
        "rsd,fd->rsf", feed_all, reduction, preferred_element_type=jnp.float32
    )
    _, pull_active = jax.vjp(activate, kept["expanded"], unit_scales)
    expanded_slope, unit_grad = pull_active(hidden_slope)
    expanded_low = expanded_slope.astype(jnp.bfloat16)
    expansion_grad = jnp.einsum(
        "rsd,rsc->dc", kept["middle_all"], expanded_low, preferred_element_type=jnp.float32
    ).reshape(width, 2, hidden_width)
    partial_middle = jnp.einsum(
        "rsc,dc->rsd",
        expanded_low,
        expansion.reshape(width, 2 * hidden_width),
        preferred_element_type=jnp.float32,
    )
    middle_total = middle_slope + lax.psum_scatter(
        partial_middle, "tensor", scatter_dimension=1, tiled=True
    )
    _, pull_branch = jax.vjp(blend, kept["stream"], kept["branch"], alphas[0])
    stream_slope, branch_slope, alpha_branch = pull_branch(middle_total)
    branch_all = lax.all_gather(branch_slope.astype(jnp.bfloat16), "tensor", axis=1, tiled=True)
    output_grad = jnp.einsum(
        "rsc,rsd->cd", kept["attended"], branch_all, preferred_element_type=jnp.float32
    )
    attended_low = jnp.einsum(
        "rsd,cd->rsc", branch_all, output_weight, preferred_element_type=jnp.float32
    ).astype(jnp.bfloat16)
    local = attended_low.shape[1]
    key_all = kept["key_all"]
    value_all = kept["value_all"]
    slots = key_all.shape[1]
    allowed, angle = placing(kept["lengths"], local)
    scores = scored(kept["query"], key_all, allowed, heads)
    probs = jnp.exp(scores - kept["log_total"])
    scale = math.sqrt(HDIM)
    back_heads = attended_low.reshape(rows, local, heads, HDIM)
    query_heads = kept["query"].reshape(rows, local, heads, HDIM)
    key_heads = key_all.reshape(rows, slots, heads, HDIM)
    value_heads = value_all.reshape(rows, slots, heads, HDIM)
    probs_slope = jnp.einsum(
        "rqhe,rkhe->rhqk", back_heads, value_heads, preferred_element_type=jnp.float32
    )
    row_term = jnp.sum(probs * probs_slope, axis=-1, keepdims=True)
    scores_low = (probs * (probs_slope - row_term)).astype(jnp.bfloat16)
    query_slope = (
        jnp.einsum("rhqk,rkhe->rqhe", scores_low, key_heads, preferred_element_type=jnp.float32)
        * scale
    )
    value_grad_all = jnp.einsum(
        "rhqk,rqhe->rkhe",
        probs.astype(jnp.bfloat16),
        back_heads,
        preferred_element_type=jnp.float32,
    )
    key_grad_all = (
        jnp.einsum("rhqk,rqhe->rkhe", scores_low, query_heads, preferred_element_type=jnp.float32)
        * scale
    )
    key_slope, value_slope = (
        lax.psum_scatter(
            key_grad_all.reshape(rows, slots, inner), "dp", scatter_dimension=1, tiled=True
        ),
        lax.psum_scatter(
            value_grad_all.reshape(rows, slots, inner), "dp", scatter_dimension=1, tiled=True
        ),
    )
    _, pull_shape = jax.vjp(
        lambda source, scale_now: shaped(source, scale_now, angle, heads),
        kept["projected"],
        query_scale,
    )
    projected_slope, query_scale_grad = pull_shape(
        (query_slope.reshape(rows, local, inner), key_slope, value_slope)
    )
    projected_low = projected_slope.astype(jnp.bfloat16)
    projection_grad = jnp.einsum(
        "rsd,rsc->dc", kept["gathered"], projected_low, preferred_element_type=jnp.float32
    ).reshape(width, 3, inner)
    partial_stream = jnp.einsum(
        "rsc,dc->rsd",
        projected_low,
        projection.reshape(width, 3 * inner),
        preferred_element_type=jnp.float32,
    )
    spread = jnp.broadcast_to(
        jnp.stack([alpha_branch, alpha_feed])[:, None, :], (2, lax.axis_size("tensor"), width)
    )
    stream_part, alpha_sum = (
        lax.psum_scatter(partial_stream, "tensor", scatter_dimension=1, tiled=True),
        lax.psum_scatter(spread, "tensor", scatter_dimension=1, tiled=True),
    )
    stream_total = stream_slope + stream_part
    return (
        stream_total,
        (
            projection_grad,
            output_grad,
            expansion_grad,
            reduction_grad,
            query_scale_grad,
            unit_grad,
            alpha_sum[:, 0],
        ),
    )


def body(
    activations,
    lengths,
    projection,
    output_weight,
    expansion,
    reduction,
    query_scale,
    unit_scales,
    alphas,
    cotangent,
):
    micro, rows, part, width = activations.shape
    section = lax.axis_index("section")
    first = section == 0
    weights = (
        projection[0],
        output_weight[0],
        expansion[0],
        reduction[0],
        query_scale[0],
        unit_scales[0],
        alphas[0],
    )
    steps = micro + 1
    received = jnp.zeros((rows, part, width), jnp.bfloat16)
    outputs = []
    keeps = []
    for step in range(steps):
        index_now = jnp.clip(step - section, 0, micro - 1)
        lengths_now = lax.dynamic_index_in_dim(lengths, index_now, 0, keepdims=False)
        stream = jnp.where(first, activations[min(step, micro - 1)], received).astype(jnp.float32)
        result, kept = forward(stream, lengths_now, weights)
        result_low = result.astype(jnp.bfloat16)
        outputs.append(result_low)
        keeps.append(kept)
        if step + 1 < steps:
            received = from_behind(result_low, "section", 1)
    stacked = jnp.stack(outputs)
    layer_output = jnp.where(first, stacked[:micro], stacked[1:])[None]
    back_received = jnp.zeros((rows, part, width), jnp.bfloat16)
    slopes = []
    summed = None
    for step in range(steps):
        batch_now = step - 1 + section
        valid = (batch_now >= 0) & (batch_now < micro)
        slope = jnp.where(first, back_received, cotangent[min(step, micro - 1)]).astype(jnp.float32)
        earlier = keeps[max(step - 1, 0)]
        later = keeps[min(step + 1, micro)]
        kept = jax.tree.map(lambda left, right: jnp.where(first, left, right), earlier, later)
        stream_total, layer_grads = backward(slope, kept, weights)
        stream_low = stream_total.astype(jnp.bfloat16)
        slopes.append(stream_low)
        masked = tuple((jnp.where(valid, piece, 0.0) for piece in layer_grads))
        summed = (
            masked
            if summed is None
            else tuple((left + right for left, right in zip(summed, masked)))
        )
        if step + 1 < steps:
            back_received = from_behind(stream_low, "section", -1)
    stacked_slopes = jnp.stack(slopes)
    input_gradient = jnp.where(first, stacked_slopes[1:], stacked_slopes[:micro])[None]
    (
        projection_grad,
        output_grad,
        expansion_grad,
        reduction_grad,
        query_scale_grad,
        unit_grad,
        alpha_grad,
    ) = summed
    totals = lax.psum(
        (
            projection_grad,
            output_grad,
            expansion_grad,
            reduction_grad,
            query_scale_grad,
            unit_grad,
            alpha_grad,
        ),
        "dp",
    )
    return (
        layer_output,
        input_gradient,
        totals[0][None],
        totals[1][None],
        totals[2][None],
        totals[3][None],
        totals[4][None],
        totals[5][None],
        totals[6][None],
    )


def solution(mesh):
    in_specs = (
        P(None, None, ("dp", "tensor"), None),
        P(),
        P("section", None, None, "tensor"),
        P("section", "tensor", None),
        P("section", None, None, "tensor"),
        P("section", "tensor", None),
        P("section", "tensor"),
        P("section", None, "tensor"),
        P("section", None, None),
        P(None, None, ("dp", "tensor"), None),
    )
    out_specs = (
        P("section", None, None, ("dp", "tensor"), None),
        P("section", None, None, ("dp", "tensor"), None),
        P("section", None, None, "tensor"),
        P("section", "tensor", None),
        P("section", None, None, "tensor"),
        P("section", "tensor", None),
        P("section", "tensor"),
        P("section", None, "tensor"),
        P("section", None, None),
    )
    return jax.shard_map(body, mesh=mesh, in_specs=in_specs, out_specs=out_specs, check_vma=False)
```

profile of v0, /device:TPU:0, one launch (start us, length us, event | category | flops | bytes accessed | tf_op | source)
XLA Modules:
  0.0 1603.8 jit_solution(17514655035893702496)
XLA Ops:
  11.8 11.5 all-gather
  56.3 16.1 %all_gather.56 = bf16[1,1024,256]{2,1,0:T(8,128)(2,1)S(1)} all-gather(bf16[1,256,256]{2,1,0:T(8,128)(2,1)S(1)} %multiply_convert_fusion.8), channel_id=1, replica_groups=mesh['section'=2,'tensor'=4,'dp'=4] {'dp'}, dimensions={1}, use_global_device_ids=true | all-gather | bytes 655360 | tf_op jit(solution)/shard_map/all_gather | solution.py:120
  75.3 16.0 all_gather.55
  103.0 5.7 copy.263
  108.7 20.8 %reduce-scatter.19.cloned.1.call-done = f32[1,64,1024]{2,1,0:T(8,128)} async-done(((f32[1,256,1024]{2,1,0:T(8,128)}), f32[1,64,1024]{2,1,0:T(8,128)}) %reduce-scatter.19.cloned.1.call-update) | async-done | bytes 262160 | tf_op jit(solution)/shard_map/reduce_scatter | solution.py:137
  131.8 10.4 all_gather.57
  150.2 27.8 %reduce-scatter.21.cloned.1.call-done = f32[1,64,1024]{2,1,0:T(8,128)} async-done(((f32[1,256,1024]{2,1,0:T(8,128)}), f32[1,64,1024]{2,1,0:T(8,128)}) %reduce-scatter.21.cloned.1.call-update) | async-done | bytes 262160 | tf_op jit(solution)/shard_map/reduce_scatter | solution.py:148
  184.1 10.4 all_gather.58
  204.4 14.9 all_gather.60
  221.9 16.5 %all_gather.59 = bf16[1,1024,256]{2,1,0:T(8,128)(2,1)S(1)} all-gather(bf16[1,256,256]{2,1,0:T(8,128)(2,1)} %slice.480), channel_id=1, replica_groups=mesh['section'=2,'tensor'=4,'dp'=4] {'dp'}, dimensions={1}, use_global_device_ids=true | all-gather | bytes 655360 | tf_op jit(solution)/shard_map/all_gather | solution.py:121
  247.0 28.4 %reduce-scatter.23.cloned.1.call-done = f32[1,64,1024]{2,1,0:T(8,128)} async-done(((f32[1,256,1024]{2,1,0:T(8,128)}), f32[1,64,1024]{2,1,0:T(8,128)}) %reduce-scatter.23.cloned.1.call-update) | async-done | bytes 262160 | tf_op jit(solution)/shard_map/reduce_scatter | solution.py:137
  277.8 10.0 all_gather.61
  295.6 27.8 %reduce-scatter.25.cloned.1.call-done = f32[1,64,1024]{2,1,0:T(8,128)} async-done(((f32[1,256,1024]{2,1,0:T(8,128)}), f32[1,64,1024]{2,1,0:T(8,128)}) %reduce-scatter.25.cloned.1.call-update) | async-done | bytes 262160 | tf_op jit(solution)/shard_map/reduce_scatter | solution.py:148
  333.2 10.5 all_gather.62
  357.2 15.8 all_gather.64
  375.7 18.1 %all_gather.63 = bf16[1,1024,256]{2,1,0:T(8,128)(2,1)} all-gather(bf16[1,256,256]{2,1,0:T(8,128)(2,1)} %slice.479), channel_id=1, replica_groups=mesh['section'=2,'tensor'=4,'dp'=4] {'dp'}, dimensions={1}, use_global_device_ids=true | all-gather | bytes 655360 | tf_op jit(solution)/shard_map/all_gather | solution.py:121
  405.0 12.5 all_gather.66
  417.5 15.8 reduce-scatter.27.cloned.1.call-done
  437.8 10.1 all_gather.65
  472.4 3.9 fusion.177
  477.5 12.0 reduce-scatter.31.cloned.1.call-done
  495.1 10.0 all_gather.67
  514.3 4.5 fusion.25
  531.4 10.1 reduce-scatter.35.cloned.1.call-done
  554.0 15.8 reduce-scatter.33.cloned.1.call-done
  574.7 24.9 %reduce-scatter.29.cloned.1.call-done = f32[1,64,1024]{2,1,0:T(8,128)} async-done(((f32[1,256,1024]{2,1,0:T(8,128)}), f32[1,64,1024]{2,1,0:T(8,128)}) %reduce-scatter.29.cloned.1.call-update) | async-done | bytes 262160 | tf_op jit(solution)/shard_map/reduce_scatter | solution.py:148
  602.3 28.6 %reduce-scatter.37.cloned.1.call-done = f32[1,64,1024]{2,1,0:T(8,128)} async-done(((f32[1,256,1024]{2,1,0:T(8,128)}), f32[1,64,1024]{2,1,0:T(8,128)}) %reduce-scatter.37.cloned.1.call-update) | async-done | bytes 262160 | tf_op jit(solution)/shard_map/reduce_scatter | solution.py:271
  640.3 10.3 all_gather.68
  660.6 3.9 fusion.178
  665.7 18.5 %reduce-scatter.39.cloned.1.call-done = f32[1,64,1024]{2,1,0:T(8,128)} async-done(((f32[1,256,1024]{2,1,0:T(8,128)}), f32[1,64,1024]{2,1,0:T(8,128)}) %reduce-scatter.39.cloned.1.call-update) | async-done | bytes 262160 | tf_op jit(solution)/shard_map/reduce_scatter | solution.py:198
  689.8 10.0 all_gather.69
  716.3 4.4 fusion.23
  720.7 15.6 reduce-scatter.43.cloned.1.call-done
  747.9 17.2 %reduce-scatter.41.cloned.1.call-done = f32[1,256,256]{1,2,0:T(8,128)} async-done(((f32[1,1024,256]{1,2,0:T(8,128)}), f32[1,256,256]{1,2,0:T(8,128)}) %reduce-scatter.41.cloned.1.call-update) | async-done | bytes 262160 | tf_op jit(solution)/shard_map/reduce_scatter | solution.py:245
  771.2 25.3 %reduce-scatter.45.cloned.1.call-done = f32[1,64,1024]{2,1,0:T(8,128)} async-done(((f32[1,256,1024]{2,1,0:T(8,128)}), f32[1,64,1024]{2,1,0:T(8,128)}) %reduce-scatter.45.cloned.1.call-update) | async-done | bytes 262160 | tf_op jit(solution)/shard_map/reduce_scatter | solution.py:271
  806.0 10.1 all_gather.70
  821.9 4.0 fusion.91
  841.6 8.1 reduce-scatter.47.cloned.1.call-done
  855.9 10.0 all_gather.71
  881.2 6.0 fusion.81
  899.7 6.3 fusion.79
  924.6 6.0 reduce-scatter.49.cloned.1.call-done
  940.0 9.2 add_bitcast_fusion
  970.7 4.4 all-reduce.44.cloned.1.call-done
  978.3 19.5 %all-reduce.36 = (f32[1,256]{1,0:T(1,128)}, f32[1,2,1024]{2,1,0:T(2,128)}, f32[1,2,1024]{2,1,0:T(2,128)}) all-reduce(f32[1,256]{1,0:T(1,128)S(1)} %bitcast.767, f32[1,2,1024]{2,1,0:T(2,128)} %add_bitcast_fusion.3, f32[1,2,1024]{2,1,0:T(2,128)} %fusion.181), channel_id=1, replica_groups=mesh['section'=2,'tensor'=4,'dp'=4] {'dp'}, use_global_device_ids=true, to_apply=%region_109.110 | all-reduce | flops 4352 | bytes 34816 | tf_op jit(solution)/shard_map/psum | solution.py:361
  997.8 8.5 reduce-scatter.53.cloned.1.call-done
  1009.0 566.1 %all-reduce.42.cloned.1.call-done = (f32[1,1024,3,256]{3,1,2,0:T(8,128)}, f32[1,256,1024]{2,1,0:T(8,128)}, f32[1,1024,2,1024]{3,1,2,0:T(8,128)}, f32[1,1024,1024]{2,1,0:T(8,128)}) async-done(((f32[1,1024,3,256]{3,1,2,0:T(8,128)}, f32[1,256,1024]{2,1,0:T(8,128)}, f32[1,1024,2,1024]{3,1,2,0:T(8,128)}, f32[1,1024,1024]{2,1,0:T(8,128)}), (f32[1,1024,3,256]{3,1,2,0:T(8,128)}, f32[1,256,1024]{2,1,0:T(8,128)}, ...) | async-done | bytes 16777232 | tf_op jit(solution)/shard_map/psum | solution.py:361
  1575.1 15.5 copy.247
  (746 shorter events, 399.4 us)
Async XLA Ops:
  7.2 141.2 %copy-start = (bf16[1,1024,1024]{2,1,0:T(8,128)(2,1)S(1)}, bf16[1,1024,1024]{2,1,0:T(8,128)(2,1)}, u32[]{:S(2)}) copy-start(bf16[1,1024,1024]{2,1,0:T(8,128)(2,1)} %param.15) | copy-start | bytes 6291460
  7.2 122.2 %reduce-scatter.19.cloned.1.call-start = ((), (), s32[]{:S(2)}) async-start(), calls=%async_computation.18 | async-start | bytes 1310720 | tf_op jit(solution)/shard_map/reduce_scatter | solution.py:137
  26.2 30.1 %copy-start.139 = (f32[1,256]{1,0:T(1,128)S(1)}, f32[1,256]{1,0:T(1,128)}, u32[]{:S(2)}) copy-start(f32[1,256]{1,0:T(1,128)} %param.16) | copy-start | bytes 3076
  72.4 25.7 %copy-start.54 = (bf16[1,1024,256]{2,1,0:T(8,128)(2,1)}, bf16[1,1024,256]{2,1,0:T(8,128)(2,1)S(1)}, u32[]{:S(2)}) copy-start(bf16[1,1024,256]{2,1,0:T(8,128)(2,1)S(1)} %all_gather.56) | copy-start | bytes 1572868
  75.3 320.6 %copy-start.138 = (f32[4,64]{1,0:T(4,128)}, f32[4,64]{1,0:T(4,128)S(1)}, u32[]{:S(2)}) copy-start(f32[4,64]{1,0:T(4,128)S(1)} %mul.2518) | copy-start | bytes 3076
  102.9 75.1 %reduce-scatter.21.cloned.1.call-start = ((), (), s32[]{:S(2)}) async-start(), calls=%async_computation.19 | async-start | bytes 1310720 | tf_op jit(solution)/shard_map/reduce_scatter | solution.py:148
  102.9 27.6 %copy-start.73 = (bf16[2,1,64,1024]{3,2,1,0:T(8,128)(2,1)S(1)}, bf16[2,1,64,1024]{3,2,1,0:T(8,128)(2,1)}, u32[]{:S(2)}) copy-start(bf16[2,1,64,1024]{3,2,1,0:T(8,128)(2,1)} %param.10) | copy-start | bytes 786436
  108.7 37.3 %copy-start.143 = (f32[1,1,1024]{2,1,0:T(1,128)}, f32[1,1,1024]{2,1,0:T(1,128)S(1)}, u32[]{:S(2)}) copy-start(f32[1,1,1024]{2,1,0:T(1,128)S(1)} %get-tuple-element.254) | copy-start | bytes 12292
  131.7 48.6 %copy-start.157 = (f32[64]{0:T(128)}, f32[64]{0:T(128)S(1)}, u32[]{:S(2)}) copy-start(f32[64]{0:T(128)S(1)} %add_rsqrt_fusion.22) | copy-start | bytes 772
  150.1 125.2 %reduce-scatter.23.cloned.1.call-start = ((), (), s32[]{:S(2)}) async-start(), calls=%async_computation.20 | async-start | bytes 1310720 | tf_op jit(solution)/shard_map/reduce_scatter | solution.py:137
  181.4 2.7 collective-permute-start
  245.6 32.1 %copy-start.136 = (bf16[4,64,256]{2,1,0:T(8,128)(2,1)}, bf16[4,64,256]{2,1,0:T(8,128)(2,1)S(1)}, u32[]{:S(2)}) copy-start(bf16[4,64,256]{2,1,0:T(8,128)(2,1)S(1)} %fusion.55) | copy-start | bytes 393220
  246.9 76.5 %reduce-scatter.25.cloned.1.call-start = ((), (), s32[]{:S(2)}) async-start(), calls=%async_computation.21 | async-start | bytes 1310720 | tf_op jit(solution)/shard_map/reduce_scatter | solution.py:148
  291.4 32.1 %copy-start.29 = (f32[1,64,1024]{2,1,0:T(8,128)S(1)}, f32[1,64,1024]{2,1,0:T(8,128)}, u32[]{:S(2)}) copy-start(f32[1,64,1024]{2,1,0:T(8,128)} %reduce-scatter.21.cloned.1.call-done) | copy-start | bytes 786436
  295.6 137.7 %reduce-scatter.27.cloned.1.call-start = ((), (), s32[]{:S(2)}) async-start(), calls=%async_computation.22 | async-start | bytes 1310720 | tf_op jit(solution)/shard_map/reduce_scatter | solution.py:137
  323.5 20.2 %copy-start.1 = (bf16[1,1024,3,256]{1,3,2,0:T(8,128)(2,1)S(1)}, bf16[1,1024,3,256]{1,3,2,0:T(8,128)(2,1)}, u32[]{:S(2)}) copy-start(bf16[1,1024,3,256]{1,3,2,0:T(8,128)(2,1)} %copy.195) | copy-start | bytes 4718596
  325.9 22.1 %copy-start.32 = (f32[1,64,1024]{2,1,0:T(8,128)}, f32[1,64,1024]{2,1,0:T(8,128)S(1)}, u32[]{:S(2)}) copy-start(f32[1,64,1024]{2,1,0:T(8,128)S(1)} %get-tuple-element.143) | copy-start | bytes 786436
  329.8 2.7 collective-permute-start.1
  351.0 44.8 %copy-start.104 = (f32[1,256,4,32]{1,3,2,0:T(8,128)}, f32[1,256,4,32]{1,3,2,0:T(8,128)S(1)}, u32[]{:S(2)}) copy-start(f32[1,256,4,32]{1,3,2,0:T(8,128)S(1)} %get-tuple-element.243) | copy-start | bytes 393220
  404.9 84.6 %reduce-scatter.31.cloned.1.call-start = ((), (), s32[]{:S(2)}) async-start(), calls=%async_computation.24 | async-start | bytes 1310720 | tf_op jit(solution)/shard_map/reduce_scatter | solution.py:198
  461.6 79.9 %reduce-scatter.35.cloned.1.call-start = ((), (), s32[]{:S(2)}) async-start(), calls=%async_computation.26 | async-start | bytes 1310720 | tf_op jit(solution)/shard_map/reduce_scatter | solution.py:242
  514.2 55.5 %reduce-scatter.33.cloned.1.call-start = ((), (), s32[]{:S(2)}) async-start(), calls=%async_computation.25 | async-start | bytes 1310720 | tf_op jit(solution)/shard_map/reduce_scatter | solution.py:245
  518.7 80.9 %reduce-scatter.29.cloned.1.call-start = ((), (), s32[]{:S(2)}) async-start(), calls=%async_computation.23 | async-start | bytes 1310720 | tf_op jit(solution)/shard_map/reduce_scatter | solution.py:148
  531.4 99.5 %reduce-scatter.37.cloned.1.call-start = ((), (), s32[]{:S(2)}) async-start(), calls=%async_computation.27 | async-start | bytes 1310720 | tf_op jit(solution)/shard_map/reduce_scatter | solution.py:271
  574.6 109.6 %reduce-scatter.39.cloned.1.call-start = ((), (), s32[]{:S(2)}) async-start(), calls=%async_computation.28 | async-start | bytes 1310720 | tf_op jit(solution)/shard_map/reduce_scatter | solution.py:198
  630.9 19.8 %copy-start.95 = (f32[1,256,2048]{2,1,0:T(8,128)S(1)}, f32[1,256,2048]{2,1,0:T(8,128)}, u32[]{:S(2)}) copy-start(f32[1,256,2048]{2,1,0:T(8,128)} %get-tuple-element.154) | copy-start | bytes 6291460
  630.9 19.8 %copy-start.146 = (f32[1,1,1024]{2,1,0:T(1,128)S(1)}, f32[1,1,1024]{2,1,0:T(1,128)}, u32[]{:S(2)}) copy-start(f32[1,1,1024]{2,1,0:T(1,128)} %copy-done.143) | copy-start | bytes 12292
  632.2 3.2 collective-permute-start.2
  656.3 27.9 %copy-start.31 = (f32[1,64,1024]{2,1,0:T(8,128)S(1)}, f32[1,64,1024]{2,1,0:T(8,128)}, u32[]{:S(2)}) copy-start(f32[1,64,1024]{2,1,0:T(8,128)} %copy-done.30) | copy-start | bytes 786436
  656.4 80.0 %reduce-scatter.43.cloned.1.call-start = ((), (), s32[]{:S(2)}) async-start(), calls=%async_computation.30 | async-start | bytes 1310720 | tf_op jit(solution)/shard_map/reduce_scatter | solution.py:242
  709.1 56.0 %reduce-scatter.41.cloned.1.call-start = ((), (), s32[]{:S(2)}) async-start(), calls=%async_computation.29 | async-start | bytes 1310720 | tf_op jit(solution)/shard_map/reduce_scatter | solution.py:245
  720.7 75.8 %reduce-scatter.45.cloned.1.call-start = ((), (), s32[]{:S(2)}) async-start(), calls=%async_computation.31 | async-start | bytes 1310720 | tf_op jit(solution)/shard_map/reduce_scatter | solution.py:271
  746.9 49.5 %copy-start.88 = (f32[1,64,1024]{2,1,0:T(8,128)S(1)}, f32[1,64,1024]{2,1,0:T(8,128)}, u32[]{:S(2)}) copy-start(f32[1,64,1024]{2,1,0:T(8,128)} %copy-done.87) | copy-start | bytes 786436
  770.0 79.8 %reduce-scatter.47.cloned.1.call-start = ((), (), s32[]{:S(2)}) async-start(), calls=%async_computation.32 | async-start | bytes 1310720 | tf_op jit(solution)/shard_map/reduce_scatter | solution.py:198
  796.5 19.7 %copy-start.147 = (f32[1,1,1024]{2,1,0:T(1,128)S(1)}, f32[1,1,1024]{2,1,0:T(1,128)}, u32[]{:S(2)}) copy-start(f32[1,1,1024]{2,1,0:T(1,128)} %copy-done.143) | copy-start | bytes 12292
  797.7 3.2 collective-permute-start.3
  821.8 92.9 %reduce-scatter.51.cloned.1.call-start = ((), (), s32[]{:S(2)}) async-start(), calls=%async_computation.34 | async-start | bytes 1310720 | tf_op jit(solution)/shard_map/reduce_scatter | solution.py:242
  827.9 21.8 %copy-start.34 = (bf16[1,64,1024]{2,1,0:T(8,128)(2,1)S(1)}, bf16[1,64,1024]{2,1,0:T(8,128)(2,1)}, u32[]{:S(2)}) copy-start(bf16[1,64,1024]{2,1,0:T(8,128)(2,1)} %copy-done.33) | copy-start | bytes 393220
  839.3 26.9 %copy-start.141 = (f32[4,256]{1,0:T(4,128)S(1)}, f32[4,256]{1,0:T(4,128)}, u32[]{:S(2)}) copy-start(f32[4,256]{1,0:T(4,128)} %get-tuple-element.248) | copy-start | bytes 12292
  874.7 55.8 %reduce-scatter.49.cloned.1.call-start = ((), (), s32[]{:S(2)}) async-start(), calls=%async_computation.33 | async-start | bytes 1310720 | tf_op jit(solution)/shard_map/reduce_scatter | solution.py:245
  894.6 80.4 %all-reduce.44.cloned.1.call-start = ((), (), s32[]{:S(2)}) async-start(), calls=%async_computation.37 | async-start | bytes 196608
  914.7 91.6 %reduce-scatter.53.cloned.1.call-start = ((), (), s32[]{:S(2)}) async-start(), calls=%async_computation.35 | async-start | bytes 1310720 | tf_op jit(solution)/shard_map/reduce_scatter | solution.py:271
  934.6 640.5 %all-reduce.42.cloned.1.call-start = ((), (), s32[]{:S(2)}) async-start(), calls=%async_computation.36 | async-start | bytes 33554432 | tf_op jit(solution)/shard_map/psum | solution.py:361
  954.1 23.0 %copy-start.153 = (f32[256,4]{0,1:T(4,128)S(1)}, f32[256,4]{0,1:T(4,128)}, u32[]{:S(2)}) copy-start(f32[256,4]{0,1:T(4,128)} %copy-done.152) | copy-start | bytes 12292
  954.1 23.2 %copy-start.110 = (f32[1,256,4,64]{1,3,2,0:T(8,128)S(1)}, f32[1,256,4,64]{1,3,2,0:T(8,128)}, u32[]{:S(2)}) copy-start(f32[1,256,4,64]{1,3,2,0:T(8,128)} %get-tuple-element.215) | copy-start | bytes 786436
  954.1 52.2 %copy-start.85 = (f32[1,64,1024]{2,1,0:T(8,128)S(1)}, f32[1,64,1024]{2,1,0:T(8,128)}, u32[]{:S(2)}) copy-start(f32[1,64,1024]{2,1,0:T(8,128)} %copy-done.84) | copy-start | bytes 786436
  954.1 53.2 %copy-start.126 = (bf16[1,64,1024]{2,1,0:T(8,128)(2,1)S(1)}, bf16[1,64,1024]{2,1,0:T(8,128)(2,1)}, u32[]{:S(2)}) copy-start(bf16[1,64,1024]{2,1,0:T(8,128)(2,1)} %copy-done.125) | copy-start | bytes 393220
  956.3 21.1 %copy-start.175 = (f32[4,64]{1,0:T(4,128)S(1)}, f32[4,64]{1,0:T(4,128)}, u32[]{:S(2)}) copy-start(f32[4,64]{1,0:T(4,128)} %get-tuple-element.67) | copy-start | bytes 3076
  (162 other events, 940.7 us)
Sparse Core Ops, SparseCore 0:
  103.0 26.3 reduce-scatter.18
  150.3 27.6 reduce-scatter.20
  247.0 28.2 reduce-scatter.22
  295.7 27.7 reduce-scatter.24
  405.0 28.2 reduce-scatter.26
  461.7 27.7 reduce-scatter.30
  514.3 27.1 reduce-scatter.34
  543.9 25.7 reduce-scatter.32
  573.2 26.3 reduce-scatter.28
  603.2 27.7 reduce-scatter.36
  656.5 27.7 reduce-scatter.38
  709.2 27.0 reduce-scatter.42
  739.2 25.7 reduce-scatter.40
  770.1 26.3 reduce-scatter.44
  822.0 27.7 reduce-scatter.46
  874.8 27.1 reduce-scatter.50
  904.7 25.7 reduce-scatter.48
  933.8 41.2 all-reduce.43
  978.5 27.7 reduce-scatter.52
  1009.9 565.1 all-reduce.41
where the time goes:
time: 1620 us; the launch traced here: 1600 us
  waiting for transfers between devices  886 us (55%)
  blocking collectives  243 us (15%)
  other arithmetic  171 us (11%)
  matrix products  144 us (9%)
  local copies, waits for them, and re-layouts  135 us (8%)
  between operations  17 us (1%)
    psum x1, waiting for transfers between devices, body(): lax.psum((projection_grad, output_grad, expansion_grad, reduction_grad, q...  566 us
    reduce_scatter x3, waiting for transfers between devices, forward(): lax.psum_scatter(partial_feed, 'tensor', scatter_dimension=1, tiled=True)  80.6 us
    reduce_scatter x3, waiting for transfers between devices, forward(): lax.psum_scatter(partial_branch, 'tensor', scatter_dimension=1, tiled=True)  64.9 us
    reduce_scatter x3, waiting for transfers between devices, backward(): lax.psum_scatter(partial_stream, 'tensor', scatter_dimension=1, tiled=True)  62.4 us
    unnamed x380, local copies, waits for them, and re-layouts  52.3 us
    all_gather x3, blocking collectives, forward(): lax.all_gather(value_low, 'dp', axis=1, tiled=True)  50.6 us
    all_gather x3, blocking collectives, forward(): lax.all_gather(key_low, 'dp', axis=1, tiled=True)  46.7 us
    reduce_scatter x3, waiting for transfers between devices, backward(): lax.psum_scatter(value_grad_all.reshape(rows, slots, inner), 'dp', scatte...  38.9 us
  transfers between devices with their start and end apart: 24, of which 23 were waited for; matrix products, arithmetic and copies ran while one was open for 13% of the time, Pallas kernels for 0%

commit v1 on v0

--- a/solution.py
+++ b/solution.py
@@ -1,8 +1,11 @@
+import functools
 import math
 
 import jax
 import jax.numpy as jnp
 from jax import lax
+from jax.experimental import pallas as pl
+from jax.experimental.pallas import tpu as pltpu
 from jax.sharding import PartitionSpec as P
 
 HDIM = 64
@@ -383,6 +386,481 @@
     )
 
 
+MESH_IDS = pl.DeviceIdType.MESH
+F32, BF16 = jnp.float32, jnp.bfloat16
+NN = ((1,), (0,))
+NT = ((1,), (1,))
+TN = ((0,), (0,))
+
+
+def dot(left, right, dims):
+    return lax.dot_general(left, right, (dims, ((), ())), preferred_element_type=F32)
+
+
+def norm_parts(v):
+    rate = lax.rsqrt(jnp.mean(v * v, axis=-1, keepdims=True) + 1e-06)
+    return v * rate, rate
+
+
+def norm_back(slope, unit, rate):
+    return rate * (slope - unit * jnp.mean(unit * slope, axis=-1, keepdims=True))
+
+
+def blend_back(slope, base, branch, alpha):
+    unit_branch, rate_branch = norm_parts(branch)
+    toward = unit_branch - base
+    unit, rate = norm_parts(base + alpha * toward)
+    inner_slope = norm_back(slope, unit, rate)
+    alpha_slope = jnp.sum(inner_slope * toward, axis=0, keepdims=True)
+    scaled = alpha * inner_slope
+    return inner_slope - scaled, norm_back(scaled, unit_branch, rate_branch), alpha_slope
+
+
+def sequence_starts(lengths_ref, row, index):
+    begin = jnp.zeros_like(index)
+    end = jnp.int32(0)
+    for sequence in range(lengths_ref.shape[2]):
+        end = end + lengths_ref[row, 0, sequence]
+        begin = jnp.where(index >= end, end, begin)
+    return jnp.where(index < end, begin, index)
+
+
+class Sizes:
+    def __init__(self, tensors, places, part, width, inner, units, sequences):
+        self.tensors, self.places, self.part, self.width = tensors, places, part, width
+        self.inner, self.units, self.sequences = inner, units, sequences
+        self.local = part * tensors
+        self.heads = inner // HDIM
+
+
+PHASES = ("stream", "heads", "mixed", "branch", "middle", "feed", "feed_low", "middle_back", "branch_low", "mixed_back", "heads_back", "stream_back")
+
+
+def relay_kernel(
+    sizes,
+    lengths_ref, acts_ref, cot_ref, qs_ref, us_ref, al_ref, wp_ref, wo_ref, we_ref, wr_ref,
+    lo_ref, ig_ref, small_ref, gp_ref, go_ref, ge_ref, gr_ref,
+    wp, wo, we, wr, qs, us, al,
+    stream, turned, rate, heads_in, probs, mixed_in, sums_in, middles, branch_f, middle_f, feed_f,
+    up_f, gate_f, hidden, feed_low, branch_low, back_in, heads_back_in,
+    heads_out, mixed_out, back_out, heads_back_out, sums_out, expanded_low,
+    outs, outs_in, grads, grad_out, key_rows, value_rows, key_grad, value_grad,
+    gp, go, ge, gr,
+    weight_sem, weight_send, send_sem, recv_sem, out_send, out_recv, grad_sem,
+):
+    T, Z, S, part = sizes.tensors, sizes.places, sizes.local, sizes.part
+    H, inner, units, D = sizes.heads, sizes.inner, sizes.units, sizes.width
+    core, t, z = lax.axis_index("section"), lax.axis_index("tensor"), lax.axis_index("dp")
+    sibling = (1 - core, t, z)
+    tensor_peers = [lax.rem(t + k, T) for k in range(1, T)]
+    place_peers = [lax.rem(z + k, Z) for k in range(1, Z)]
+    tensor_ids = [(core, peer, z) for peer in tensor_peers]
+    place_ids = [(core, t, peer) for peer in place_peers]
+    pending = []
+
+    own_weights = [(wp_ref, wp), (wo_ref, wo), (we_ref, we), (wr_ref, wr)]
+    for piece, (source, target) in enumerate(own_weights):
+        pltpu.make_async_copy(source, target.at[core], weight_sem.at[core, piece]).start()
+    small_weights = [(qs_ref, qs), (us_ref, us), (al_ref, al)]
+    for piece, (source, target) in enumerate(small_weights):
+        pltpu.make_async_copy(source, target.at[core], weight_sem.at[core, 4 + piece]).start()
+
+    barrier = pltpu.get_barrier_semaphore()
+    partners = [sibling] + tensor_ids + place_ids
+    for partner in partners:
+        pl.semaphore_signal(barrier, inc=1, device_id=partner, device_id_type=MESH_IDS)
+    pl.semaphore_wait(barrier, len(partners))
+
+    for piece, (source, target) in list(enumerate(small_weights, 4)) + list(enumerate(own_weights)):
+        copy = pltpu.make_async_remote_copy(
+            source, target.at[core], weight_send.at[piece], weight_sem.at[core, piece], device_id=sibling, device_id_type=MESH_IDS
+        )
+        copy.start()
+        pending.append(copy)
+
+    def await_weight(layer, piece):
+        source, target = (own_weights + small_weights)[piece]
+        pltpu.make_async_copy(source, target.at[layer], weight_sem.at[layer, piece]).wait()
+
+    def exchange(layer, phase, ids, sources, targets):
+        number = layer * len(PHASES) + PHASES.index(phase)
+        copies = []
+        for k, device in enumerate(ids):
+            copy = pltpu.make_async_remote_copy(
+                sources[k], targets[k], send_sem.at[number, k], recv_sem.at[number, k], device_id=device, device_id_type=MESH_IDS
+            )
+            copy.start()
+            copies.append(copy)
+        pending.extend(copies)
+        return copies
+
+    def arrive(copies):
+        for copy in copies:
+            copy.wait_recv()
+
+    my_rows = pl.ds(pl.multiple_of(t * part, part), part)
+
+    def gather(layer, phase, target, value):
+        target[layer, my_rows, :] = value
+        mine = target.at[layer, my_rows, :]
+        return exchange(layer, phase, tensor_ids, [mine] * (T - 1), [mine] * (T - 1))
+
+    def scatter(layer, phase, number):
+        return exchange(
+            layer, phase, tensor_ids, [sums_out.at[layer, number, peer] for peer in tensor_peers], [sums_in.at[layer, number, k] for k in range(T - 1)]
+        )
+
+    def scattered(layer, number, copies):
+        arrive(copies)
+        total = sums_out[layer, number, t].astype(F32)
+        for k in range(T - 1):
+            total = total + sums_in[layer, number, k].astype(F32)
+        return total
+
+    def spread(layer, phase, source, target):
+        target[layer, z] = source[layer, z]
+        return exchange(layer, phase, place_ids, [source.at[layer, peer] for peer in place_peers], [target.at[layer, z]] * (Z - 1))
+
+    index_all = lax.broadcasted_iota(jnp.int32, (1, S * Z), 1)
+    index_here = lax.broadcasted_iota(jnp.int32, (1, S), 1) + z * S
+    starts = sequence_starts(lengths_ref, core, index_all)
+    position = (index_here - sequence_starts(lengths_ref, core, index_here)).astype(F32)
+    half = HDIM // 2
+    rates = jnp.exp(lax.broadcasted_iota(jnp.int32, (half, 1), 0).astype(F32) * (-2.0 * math.log(10000.0) / HDIM))
+    angle = rates * position
+    cosine, sine = jnp.cos(angle)[None], jnp.sin(angle)[None]
+    key_index = lax.broadcasted_iota(jnp.int32, (S * Z, S), 0)
+
+    def rotate_heads(v):
+        front, back = v[:, :half], v[:, half:]
+        return jnp.concatenate([front * cosine - back * sine, back * cosine + front * sine], axis=1)
+
+    def rotate_back(v):
+        front, back = v[:, :half], v[:, half:]
+        return jnp.concatenate([front * cosine + back * sine, back * cosine - front * sine], axis=1)
+
+    def column(row):
+        return jnp.broadcast_to(row, (8, row.shape[1])).T[:, :1]
+
+    def block(query, key):
+        return query * (query + 1) // 2 + key
+
+    def forward(layer, base_low):
+        copies = gather(layer, "stream", stream, base_low)
+        await_weight(layer, 0)
+        await_weight(layer, 4)
+        await_weight(layer, 5)
+        await_weight(layer, 6)
+        scale = column(qs[layer]).reshape(H, HDIM, 1)
+        base = base_low.astype(F32)
+        arrive(copies)
+        gathered = stream[layer]
+        for third in range(3):
+            piece = dot(gathered, wp[layer, third], NN).T.reshape(H, HDIM, S)
+            if third < 2:
+                piece = rotate_heads(piece)
+                speed = lax.rsqrt(jnp.sum(piece * piece, axis=1, keepdims=True) + 1e-06)
+                piece = piece * speed
+                turned[layer, third] = piece
+                rate[layer, third] = speed
+                piece = piece * scale
+            heads_out[layer, :, third] = piece.astype(BF16)
+        copies = spread(layer, "heads", heads_out, heads_in)
+        arrive(copies)
+        for place in range(Z):
+            key_rows[place] = heads_in[layer, place, 1].T
+        for query in range(Z):
+            count = (query + 1) * S
+            raw = [
+                dot(key_rows[key], heads_in[layer, query, 0], NN) * math.sqrt(HDIM) for key in range(query + 1)
+            ]
+            first = starts[:, query * S : count]
+            last = index_all[:, query * S : count]
+            scores = []
+            for key in range(query + 1):
+                keys = key_index[key * S : (key + 1) * S]
+                allowed = keys >= first
+                if key == query:
+                    allowed = allowed & (keys <= last)
+                scores.append(jnp.where(allowed, raw[key], -1e30))
+            highest = scores[0].max(axis=0, keepdims=True)
+            for piece in scores[1:]:
+                highest = jnp.maximum(highest, piece.max(axis=0, keepdims=True))
+            lifted = [jnp.exp(piece - highest) for piece in scores]
+            total = lifted[0].sum(axis=0, keepdims=True)
+            for piece in lifted[1:]:
+                total = total + piece.sum(axis=0, keepdims=True)
+            shrink = 1.0 / total
+            mixed = None
+            for key in range(query + 1):
+                low = (lifted[key] * shrink).astype(BF16)
+                probs[layer, block(query, key)] = low
+                term = dot(heads_in[layer, key, 2], low, NN)
+                mixed = term if mixed is None else mixed + term
+            mixed_out[layer, query] = mixed.astype(BF16)
+        copies = spread(layer, "mixed", mixed_out, mixed_in)
+        await_weight(layer, 1)
+        arrive(copies)
+        attended = mixed_in[layer].reshape(inner, S).T
+        partial = dot(attended, wo[layer], NN)
+        sums_out[layer, 0] = partial.astype(BF16).reshape(T, part, D)
+        branch = scattered(layer, 0, scatter(layer, "branch", 0))
+        branch_f[layer] = branch
+        alpha = al[layer]
+        middle = norm_parts(base + alpha[0:1] * (norm_parts(branch)[0] - base))[0]
+        middle_f[layer] = middle
+        copies = gather(layer, "middle", middles, middle.astype(BF16))
+        await_weight(layer, 2)
+        arrive(copies)
+        middle_all = middles[layer]
+        step = 256
+        for begin in range(0, units, step):
+            cols = slice(begin, begin + step)
+            up = dot(middle_all, we[layer, 0, :, cols], NN)
+            gate = dot(middle_all, we[layer, 1, :, cols], NN)
+            up_f[layer, :, cols] = up
+            gate_f[layer, :, cols] = gate
+            inside = us[layer, 1:2, cols] * gate
+            hidden[layer, :, cols] = (us[layer, 0:1, cols] * up * (inside / (1.0 + jnp.exp(-inside)))).astype(BF16)
+        await_weight(layer, 3)
+        acted = hidden[layer]
+        for begin in range(0, D, step):
+            cols = slice(begin, begin + step)
+            sums_out[layer, 1, :, :, cols] = dot(acted, wr[layer, :, cols], NN).astype(BF16).reshape(T, part, step)
+        feed = scattered(layer, 1, scatter(layer, "feed", 1))
+        feed_f[layer] = feed
+        result = norm_parts(middle + alpha[1:2] * (norm_parts(feed)[0] - middle))[0].astype(BF16)
+        outs[0, layer] = result
+        return result
+
+    def backward(layer, base_low, slope):
+        alpha = al[layer]
+        middle_slope, feed_slope, alpha_m = blend_back(slope, middle_f[layer], feed_f[layer], alpha[1:2])
+        arrive(gather(layer, "feed_low", feed_low, feed_slope.astype(BF16)))
+        small_ref[layer, 1:2] = alpha_m
+        feed_all = feed_low[layer]
+        step = 256
+        for begin in range(0, units, step):
+            cols = slice(begin, begin + step)
+            slope_hidden = dot(feed_all, wr[layer, cols, :], NT)
+            up, gate = up_f[layer, :, cols], gate_f[layer, :, cols]
+            scale_up, scale_gate = us[layer, 0:1, cols], us[layer, 1:2, cols]
+            inside = scale_gate * gate
+            sigmoid = 1.0 / (1.0 + jnp.exp(-inside))
+            silu = inside * sigmoid
+            silu_slope = sigmoid + silu * (1.0 - sigmoid)
+            by_up = silu * slope_hidden
+            by_gate = scale_up * up * silu_slope * slope_hidden
+            small_ref[layer, 2:3, cols] = jnp.sum(by_up * up, axis=0, keepdims=True)
+            small_ref[layer, 3:4, cols] = jnp.sum(by_gate * gate, axis=0, keepdims=True)
+            expanded_low[layer, 0, :, cols] = (by_up * scale_up).astype(BF16)
+            expanded_low[layer, 1, :, cols] = (by_gate * scale_gate).astype(BF16)
+        for begin in range(0, D, step):
+            rows = slice(begin, begin + step)
+            partial = dot(expanded_low[layer, 0], we[layer, 0, rows, :], NT) + dot(expanded_low[layer, 1], we[layer, 1, rows, :], NT)
+            sums_out[layer, 2, :, :, rows] = partial.astype(BF16).reshape(T, part, step)
+        copies = scatter(layer, "middle_back", 2)
+        middle_cols = middles[layer].T
+        hidden_cols = hidden[layer].T
+        slot = lax.rem(core + layer, 2)
+        for begin in range(0, units, step):
+            cols = slice(begin, begin + step)
+            for side in range(2):
+                ge[side, :, cols] = dot(middle_cols, expanded_low[layer, side, :, cols], NN).astype(BF16)
+            gr[:, cols] = dot(hidden_cols, feed_all[:, cols], NN).astype(BF16)
+        started = [
+            pltpu.make_async_copy(ge, ge_ref.at[slot], grad_sem.at[layer, 0]),
+            pltpu.make_async_copy(gr, gr_ref.at[slot], grad_sem.at[layer, 1]),
+        ]
+        for copy in started:
+            copy.start()
+        middle_total = middle_slope + scattered(layer, 2, copies)
+        stream_slope, branch_slope, alpha_a = blend_back(middle_total, base_low.astype(F32), branch_f[layer], alpha[0:1])
+        arrive(gather(layer, "branch_low", branch_low, branch_slope.astype(BF16)))
+        small_ref[layer, 0:1] = alpha_a
+        branch_all = branch_low[layer]
+        back_out[layer] = dot(wo[layer], branch_all, NT).astype(BF16).reshape(H, HDIM, S)
+        copies = spread(layer, "mixed_back", back_out, back_in)
+        go[...] = dot(mixed_in[layer].reshape(inner, S), branch_all, NN).astype(BF16)
+        copy = pltpu.make_async_copy(go, go_ref.at[slot], grad_sem.at[layer, 2])
+        copy.start()
+        started.append(copy)
+        for place in range(Z):
+            value_rows[place] = heads_in[layer, place, 2].T
+        arrive(copies)
+        for query in range(Z):
+            slope_mixed = back_in[layer, query]
+            lows = [probs[layer, block(query, key)] for key in range(query + 1)]
+            probs_slope = [dot(value_rows[key], slope_mixed, NN) for key in range(query + 1)]
+            row_term = None
+            for low, piece in zip(lows, probs_slope):
+                term = jnp.sum(low.astype(F32) * piece, axis=0, keepdims=True)
+                row_term = term if row_term is None else row_term + term
+            query_slope = None
+            for key in range(query + 1):
+                low = lows[key]
+                scores_low = (low.astype(F32) * (probs_slope[key] - row_term)).astype(BF16)
+                term = dot(heads_in[layer, key, 1], scores_low, NN)
+                query_slope = term if query_slope is None else query_slope + term
+                key_term = dot(heads_in[layer, query, 0], scores_low, NT)
+                value_term = dot(slope_mixed, low, NT)
+                if key == query:
+                    key_grad[key] = key_term
+                    value_grad[key] = value_term
+                else:
+                    key_grad[key] += key_term
+                    value_grad[key] += value_term
+            heads_back_out[layer, query, 0] = (query_slope * math.sqrt(HDIM)).astype(BF16)
+        for place in range(Z):
+            heads_back_out[layer, place, 1] = (key_grad[place] * math.sqrt(HDIM)).astype(BF16)
+            heads_back_out[layer, place, 2] = value_grad[place].astype(BF16)
+        copies = spread(layer, "heads_back", heads_back_out, heads_back_in)
+        scale = column(qs[layer]).reshape(H, HDIM, 1)
+        stream_cols = stream[layer].T
+        arrive(copies)
+        scale_slope = None
+        lows = []
+        for third in range(3):
+            piece = heads_back_in[layer, :, third]
+            if third < 2:
+                piece = piece.astype(F32)
+                unit = turned[layer, third]
+                term = jnp.sum(piece * unit, axis=2, keepdims=True)
+                scale_slope = term if scale_slope is None else scale_slope + term
+                piece = piece * scale
+                piece = rate[layer, third] * (piece - unit * jnp.sum(unit * piece, axis=1, keepdims=True))
+                piece = rotate_back(piece).astype(BF16)
+            lows.append(piece.reshape(inner, S).T)
+        partial = None
+        for third in range(3):
+            term = dot(lows[third], wp[layer, third], NT)
+            partial = term if partial is None else partial + term
+        sums_out[layer, 3] = partial.astype(BF16).reshape(T, part, D)
+        copies = scatter(layer, "stream_back", 3)
+        small_ref[layer, 4:5, :inner] = jnp.broadcast_to(scale_slope.reshape(inner, 1), (inner, 128)).T[:1]
+        for third in range(3):
+            gp[third] = dot(stream_cols, lows[third], NN).astype(BF16)
+        copy = pltpu.make_async_copy(gp, gp_ref.at[slot], grad_sem.at[layer, 3])
+        copy.start()
+        started.append(copy)
+        result = (stream_slope + scattered(layer, 3, copies)).astype(BF16)
+        outs[1, layer] = result
+        for copy in started:
+            copy.wait()
+        return result
+
+    small_ref[...] = jnp.zeros_like(small_ref)
+    base_first = acts_ref[core, 0]
+    first = forward(0, base_first)
+    forward(1, first)
+    slope = backward(1, outs[0, 0], cot_ref[core, 0].astype(F32))
+    backward(0, acts_ref[core, 0], slope.astype(F32))
+
+    other = 1 - core
+    copy = pltpu.make_async_remote_copy(
+        outs.at[:, other], outs_in, out_send, out_recv, device_id=sibling, device_id_type=MESH_IDS
+    )
+    copy.start()
+    for kind, target in enumerate((lo_ref, ig_ref)):
+        target[core] = outs[kind, core]
+    copy.wait_recv()
+    for kind, target in enumerate((lo_ref, ig_ref)):
+        target[other] = outs_in[kind]
+    copy.wait_send()
+    for copy in pending:
+        copy.wait_send()
+
+
+def relay(sizes, lengths, acts, cot, qs, us, al, wp, wo, we, wr):
+    T, Z, S, part = sizes.tensors, sizes.places, sizes.local, sizes.part
+    H, inner, units, D = sizes.heads, sizes.inner, sizes.units, sizes.width
+    blocks = Z * (Z + 1) // 2
+    vmem = pl.BlockSpec(memory_space=pltpu.VMEM)
+    hbm = pl.BlockSpec(memory_space=pl.ANY)
+    out_shape = (
+        jax.ShapeDtypeStruct((2, part, D), BF16),
+        jax.ShapeDtypeStruct((2, part, D), BF16),
+        jax.ShapeDtypeStruct((2, 8, D), F32),
+        jax.ShapeDtypeStruct((2, 3, D, inner), BF16),
+        jax.ShapeDtypeStruct((2, inner, D), BF16),
+        jax.ShapeDtypeStruct((2, 2, D, units), BF16),
+        jax.ShapeDtypeStruct((2, units, D), BF16),
+    )
+    DMA = pltpu.SemaphoreType.DMA
+    V = pltpu.VMEM
+    scratch = [
+        V((2, 3, D, inner), BF16), V((2, inner, D), BF16), V((2, 2, D, units), BF16), V((2, units, D), BF16),
+        V((2, 1, inner), F32), V((2, 2, units), F32), V((2, 2, D), F32),
+        V((2, S, D), BF16),
+        V((2, 2, H, HDIM, S), F32),
+        V((2, 2, H, 1, S), F32),
+        V((2, Z, 3, HDIM, S), BF16),
+        V((2, blocks, S, S), BF16),
+        V((2, H, HDIM, S), BF16),
+        V((2, 4, T - 1, part, D), BF16),
+        V((2, S, D), BF16),
+        V((2, part, D), F32), V((2, part, D), F32), V((2, part, D), F32),
+        V((2, S, units), F32), V((2, S, units), F32),
+        V((2, S, units), BF16),
+        V((2, S, D), BF16), V((2, S, D), BF16),
+        V((2, Z, HDIM, S), BF16),
+        V((2, H, 3, HDIM, S), BF16),
+        V((2, H, 3, HDIM, S), BF16),
+        V((2, Z, HDIM, S), BF16),
+        V((2, H, HDIM, S), BF16),
+        V((2, Z, 3, HDIM, S), BF16),
+        V((2, 4, T, part, D), BF16),
+        V((2, 2, S, units), BF16),
+        V((2, 2, part, D), BF16), V((2, part, D), BF16),
+        V((8, 128), F32), V((8, 128), F32),
+        V((Z, S, HDIM), BF16), V((Z, S, HDIM), BF16),
+        V((Z, HDIM, S), F32), V((Z, HDIM, S), F32),
+        V((3, D, inner), BF16), V((inner, D), BF16), V((2, D, units), BF16), V((units, D), BF16),
+        DMA((2, 7)), DMA((7,)), DMA((2 * len(PHASES), 3)), DMA((2 * len(PHASES), 3)), DMA, DMA, DMA((2, 4)),
+    ]
+    return pl.pallas_call(
+        functools.partial(relay_kernel, sizes),
+        out_shape=out_shape,
+        in_specs=[pl.BlockSpec(memory_space=pltpu.SMEM), vmem, vmem, vmem, vmem, vmem, hbm, hbm, hbm, hbm],
+        out_specs=(vmem, vmem, vmem, hbm, hbm, hbm, hbm),
+        scratch_shapes=scratch,
+        compiler_params=pltpu.CompilerParams(collective_id=0, has_side_effects=True, vmem_limit_bytes=60 * 2**20),
+        name="relay",
+    )(lengths, acts, cot, qs, us, al, wp, wo, we, wr)
+
+
+def fast_body(
+    activations, lengths, projection, output_weight, expansion, reduction, query_scale, unit_scales, alphas, cotangent
+):
+    _, _, part, width = activations.shape
+    inner, units = output_weight.shape[1], reduction.shape[1]
+    sizes = Sizes(lax.axis_size("tensor"), lax.axis_size("dp"), part, width, inner, units, lengths.shape[2])
+    core = lax.axis_index("section")
+    lo, ig, small, gp, go, ge, gr = relay(
+        sizes, lengths, activations, cotangent, query_scale, unit_scales[0], alphas[0],
+        projection[0].transpose(1, 0, 2), output_weight[0], expansion[0].transpose(1, 0, 2), reduction[0],
+    )
+
+    def total(pair):
+        got = lax.ppermute(pair[1], "section", [(0, 1), (1, 0)])
+        return lax.psum((pair[0].astype(F32) + got.astype(F32)).astype(BF16), "dp").astype(F32)
+
+    small = lax.psum(small, ("section", "dp"))
+    small = lax.dynamic_index_in_dim(small, core, 0, keepdims=False)
+    alpha_grad = lax.psum(small[0:2], "tensor")
+    return (
+        lo[None, :, None],
+        ig[None, :, None],
+        total(gp).transpose(1, 0, 2)[None],
+        total(go)[None],
+        total(ge).transpose(1, 0, 2)[None],
+        total(gr)[None],
+        small[4:5, :inner],
+        small[None, 2:4, :units],
+        alpha_grad[None],
+    )
+
+
 def solution(mesh):
     in_specs = (
         P(None, None, ("dp", "tensor"), None),
@@ -407,4 +885,16 @@
         P("section", None, "tensor"),
         P("section", None, None),
     )
-    return jax.shard_map(body, mesh=mesh, in_specs=in_specs, out_specs=out_specs, check_vma=False)
+    def chosen(*arrays):
+        activations, output_weight = arrays[0], arrays[3]
+        heads = output_weight.shape[1] // HDIM
+        fits = (
+            mesh.shape["section"] == 2
+            and mesh.shape["tensor"] == 4
+            and mesh.shape["dp"] == heads
+            and activations.shape[:2] == (2, 1)
+            and activations.shape[2] * mesh.shape["tensor"] == 256
+        )
+        return (fast_body if fits else body)(*arrays)
+
+    return jax.shard_map(chosen, mesh=mesh, in_specs=in_specs, out_specs=out_specs, check_vma=False)

time: 1620 us -> 599 us (0.37)
  waiting for transfers between devices: 886 us -> 319 us
  blocking collectives: 243 us -> 10.8 us
  Pallas kernels: 0 us -> 190 us
  other arithmetic: 171 us -> 24.6 us
  matrix products: 144 us -> 0 us
  local copies, waits for them, and re-layouts: 135 us -> 28.8 us
    reduce_scatter x18 -> x0, waiting for transfers between devices: 311 us -> none  [the longest x3 80.6 us: forward(): lax.psum_scatter(partial_feed, 'tensor', scatter_dimension=1, tiled=True)]
    psum x1 -> x2, waiting for transfers between devices: 566 us -> 311 us  [the longest x1 282 us: total(): lax.psum((pair[0].astype(F32) + got.astype(F32)).astype(BF16), 'dp')]
    all_gather x18 -> x0, blocking collectives: 223 us -> none  [the longest x3 50.6 us: forward(): lax.all_gather(value_low, 'dp', axis=1, tiled=True)]
    pallas_call x0 -> x1, Pallas kernels: none -> 190 us  [relay(): pl.pallas_call(functools.partial(relay_kernel, sizes), out_shape=out_shap...]
    dot_general x57 -> x0, matrix products: 144 us -> none  [the longest x3 21.6 us: backward(): jnp.einsum('rsd,rsc->dc', kept['middle_all'], expanded_low, preferred_ele...]
    reduce_sum x46 -> x0, other arithmetic: 56.5 us -> none  [the longest x16 24.1 us: normed(): return v * lax.rsqrt(jnp.mean(v * v, axis=-1, keepdims=True) + 1e-06)]
    unnamed x380 -> x18, local copies, waits for them, and re-layouts: 52.3 us -> 17.6 us
    slice x29 -> x2, local copies, waits for them, and re-layouts: 27.1 us -> 2 us  [the longest x1 1.44 us: fast_body(): alpha_grad = lax.psum(small[0:2], 'tensor')]
  transfers between devices with their start and end apart: 24 -> 6, of which waited for: 23 -> 3; matrix products, arithmetic and copies ran while one was open for 13% -> 4% of each run, Pallas kernels for 0% -> 0%
where the time goes in v1:
time: 599 us; the launch traced here: 589 us
  waiting for transfers between devices  319 us (53%)
  Pallas kernels  190 us (32%)
  local copies, waits for them, and re-layouts  28.8 us (5%)
  other arithmetic  24.6 us (4%)
  between operations  14.5 us (2%)
  blocking collectives  10.8 us (2%)
    psum x1, waiting for transfers between devices, total(): lax.psum((pair[0].astype(F32) + got.astype(F32)).astype(BF16), 'dp')  282 us
    pallas_call x1, Pallas kernels, relay(): pl.pallas_call(functools.partial(relay_kernel, sizes), out_shape=out_shap...  190 us
    psum x1, waiting for transfers between devices, fast_body(): small = lax.psum(small, ('section', 'dp'))  28.8 us
    unnamed x18, local copies, waits for them, and re-layouts  17.6 us
  transfers between devices with their start and end apart: 6, of which 3 were waited for; matrix products, arithmetic and copies ran while one was open for 4% of the time, Pallas kernels for 0%

profile of v1, /device:TPU:0, one launch (start us, length us, event | category | flops | bytes accessed | tf_op | source)
XLA Modules:
  0.0 588.9 jit_solution(8012587654737325310)
XLA Ops:
  7.2 0.0 all-reduce.4.cloned.1.call-start
  7.2 5.5 copy.24
  12.7 189.9 %relay.1 = (bf16[2,64,1024]{2,1,0:T(8,128)(2,1)}, bf16[2,64,1024]{2,1,0:T(8,128)(2,1)}, f32[2,8,1024]{2,1,0:T(8,128)}, bf16[2,3,1024,256]{3,2,1,0:T(8,128)(2,1)}...) custom-call(s32[2,1,8]{2,1,0:T(1,128)} %lengths_ref.1, ...), custom_call_target="tpu_custom_call" | custom-call | tf_op jit(solution)/shard_map/relay/pallas_call | solution.py:821
  202.7 0.0 copy-start
  202.7 4.8 slice_bitcast_fusion
  207.5 0.0 copy-start.2
  207.5 0.4 collective-permute-start.2
  207.9 0.0 copy-done
  207.9 0.0 copy-start.4
  207.9 1.5 slice_bitcast_fusion.1
  209.4 0.1 collective-permute-start.3
  209.5 0.6 copy-done.2
  210.1 1.2 slice_bitcast_fusion.2
  211.4 0.4 collective-permute-start
  211.8 0.0 copy-done.4
  211.8 0.8 slice_bitcast_fusion.3
  212.6 0.1 collective-permute-start.1
  212.7 0.0 all-reduce.4.cloned.1.call-update
  212.7 0.0 all-reduce.6.cloned.1.call-start
  212.8 0.0 copy-start.1
  212.8 8.2 %collective-permute-done.1 = bf16[256,1024]{1,0:T(8,128)(2,1)} collective-permute-done((bf16[256,1024]{1,0:T(8,128)(2,1)}, bf16[256,1024]{1,0:T(8,128)(2,1)}, u32[]{:S(2)}, u32[]{:S(2)}) %collective-permute-start.1) | collective-permute-done | bytes 524320 | tf_op jit(solution)/shard_map/ppermute | solution.py:845
  221.0 2.2 fusion.7
  223.2 0.0 collective-permute-done
  223.2 2.9 fusion.5
  226.1 0.0 collective-permute-done.3
  226.1 0.0 copy-done.1
  226.1 3.9 fusion.4
  230.0 0.0 collective-permute-done.2
  230.0 7.6 %fusion.1 = bf16[1,1024,2,1024]{3,1,2,0:T(8,128)(2,1)} fusion(bf16[2,1024,1024]{2,1,0:T(8,128)(2,1)} %collective-permute-done.2, bf16[2,2,1024,1024]{3,2,1,0:T(8,128)(2,1)} %get-tuple-element.20), kind=kLoop, calls=%fused_computation.2 | loop fusion | flops 8388608 | bytes 12582912 | tf_op jit(solution)/shard_map/broadcast_in_dim | solution.py:856
  237.6 0.0 all-reduce.6.cloned.1.call-update
  237.7 28.8 %all-reduce.4.cloned.1.call-done = f32[2,8,1024]{2,1,0:T(8,128)} async-done(((f32[2,8,1024]{2,1,0:T(8,128)}), f32[2,8,1024]{2,1,0:T(8,128)}) %all-reduce.4.cloned.1.call-update) | async-done | bytes 65552 | tf_op jit(solution)/shard_map/psum | solution.py:848
  266.5 0.8 dynamic-slice_bitcast_fusion
  267.2 0.6 slice.49
  267.8 1.4 constant_dynamic-slice_fusion
  269.2 10.8 %psum.47 = f32[1,2,1024]{2,1,0:T(2,128)} all-reduce(f32[1,2,1024]{2,1,0:T(2,128)S(1)} %get-tuple-element.36), channel_id=1, replica_groups=mesh['section'=2,'tensor'=4,'dp'=4] {'tensor'}, use_global_device_ids=true, to_apply=%region_5.6 | all-reduce | flops 2048 | bytes 16384 | tf_op jit(solution)/shard_map/psum | solution.py:850
  280.0 282.2 %all-reduce.6.cloned.1.call-done = (bf16[1,1024,2,1024]{3,1,2,0:T(8,128)(2,1)}, bf16[1,1024,3,256]{3,1,2,0:T(8,128)(2,1)}, bf16[1,256,1024]{2,1,0:T(8,128)(2,1)}, bf16[1,1024,1024]{2,1,0:T(8,128)(2,1)}) async-done(((bf16[1,1024,2,1024]{3,1,2,0:T(8,128)(2,1)}, bf16[1,1024,3,256]{3,1,2,0:T(8,128)(2,1)}, bf16[1,256,1024]{2,1,0:T(8,128)(2,1)}, bf16[1,1024,1024]{2,1,0:T(8,128)(2,1)}), ...) | async-done | bytes 8388624 | tf_op jit(solution)/shard_map/psum | solution.py:846
  562.2 2.1 broadcast_in_dim.39
  564.3 3.3 broadcast_in_dim.37
  567.7 0.0 copy-start.3
  567.7 10.0 %copy.22 = f32[1,1024,2,1024]{3,2,1,0:T(2,128)} copy(bf16[1,1024,2,1024]{3,1,2,0:T(8,128)(2,1)} %get-tuple-element.32) | data formatting | bytes 12582912
  577.7 0.0 copy-done.3
  577.7 0.0 copy-start.6
  577.7 0.0 copy-start.5
  577.7 2.5 broadcast_in_dim.43
  580.2 0.0 copy-done.6
  580.2 0.7 copy.32
  580.9 0.0 copy-done.5
  580.9 0.7 copy.33
Async XLA Ops:
  7.2 259.3 %all-reduce.4.cloned.1.call-start = ((), (), s32[]{:S(2)}) async-start(), calls=%async_computation | async-start | bytes 131072 | tf_op jit(solution)/shard_map/psum | solution.py:848
  202.7 5.2 copy-start
  207.5 2.6 copy-start.2
  207.5 22.5 %collective-permute-start.2 = (bf16[2,1024,1024]{2,1,0:T(8,128)(2,1)}, bf16[2,1024,1024]{2,1,0:T(8,128)(2,1)}, u32[]{:S(2)}, u32[]{:S(2)}) collective-permute-start(bf16[2,1024,1024]{2,1,0:T(8,128)(2,1)} %slice_bitcast_fusion), channel_id=1, source_target_pairs={{0,16},{16,0},{1,17},{17,1},{2,18},{18,2},{3,19},{19,3},{4,20},{20... | collective-permute-start | bytes 12582920 | tf_op jit(solution)/shard_map/ppermute | solution.py:845
  207.9 3.9 copy-start.4
  209.4 16.7 %collective-permute-start.3 = (bf16[1024,1024]{1,0:T(8,128)(2,1)}, bf16[1024,1024]{1,0:T(8,128)(2,1)}, u32[]{:S(2)}, u32[]{:S(2)}) collective-permute-start(bf16[1024,1024]{1,0:T(8,128)(2,1)} %slice_bitcast_fusion.1), channel_id=1, source_target_pairs={{0,16},{16,0},{1,17},{17,1},{2,18},{18,2},{3,19},{19,3},{4,20},{20... | collective-permute-start | bytes 6291464 | tf_op jit(solution)/shard_map/ppermute | solution.py:845
  211.4 11.8 %collective-permute-start = (bf16[3,1024,256]{2,1,0:T(8,128)(2,1)}, bf16[3,1024,256]{2,1,0:T(8,128)(2,1)}, u32[]{:S(2)}, u32[]{:S(2)}) collective-permute-start(bf16[3,1024,256]{2,1,0:T(8,128)(2,1)} %slice_bitcast_fusion.2), channel_id=1, source_target_pairs={{0,16},{16,0},{1,17},{17,1},{2,18},{18,2},{3,19},{19,3},{4,20},{20... | collective-permute-start | bytes 4718600 | tf_op jit(solution)/shard_map/ppermute | solution.py:845
  212.6 8.4 %collective-permute-start.1 = (bf16[256,1024]{1,0:T(8,128)(2,1)}, bf16[256,1024]{1,0:T(8,128)(2,1)}, u32[]{:S(2)}, u32[]{:S(2)}) collective-permute-start(bf16[256,1024]{1,0:T(8,128)(2,1)} %slice_bitcast_fusion.3), channel_id=1, source_target_pairs={{0,16},{16,0},{1,17},{17,1},{2,18},{18,2},{3,19},{19,3},{4,20},{20... | collective-permute-start | bytes 1572872 | tf_op jit(solution)/shard_map/ppermute | solution.py:845
  212.7 349.4 %all-reduce.6.cloned.1.call-start = ((), (), s32[]{:S(2)}) async-start(), calls=%async_computation.1 | async-start | bytes 16777216 | tf_op jit(solution)/shard_map/psum | solution.py:846
  212.8 13.3 %copy-start.1 = (bf16[2,1024,1024]{2,1,0:T(8,128)(2,1)S(1)}, bf16[2,1024,1024]{2,1,0:T(8,128)(2,1)}, u32[]{:S(2)}) copy-start(bf16[2,1024,1024]{2,1,0:T(8,128)(2,1)} %get-tuple-element.21) | copy-start | bytes 12582916
  567.7 10.0 %copy-start.3 = (bf16[1,1024,1024]{2,1,0:T(8,128)(2,1)S(1)}, bf16[1,1024,1024]{2,1,0:T(8,128)(2,1)}, u32[]{:S(2)}) copy-start(bf16[1,1024,1024]{2,1,0:T(8,128)(2,1)} %get-tuple-element.35) | copy-start | bytes 6291460
  577.7 2.5 copy-start.6
  577.7 3.2 copy-start.5
Sparse Core Ops, SparseCore 0:
  212.9 53.5 all-reduce.3
  270.2 291.9 all-reduce.5
